TPU v7x, 32 devices: a whole 2x2x4 slice. The times are simulated.
32 devices in a mesh: inner: 16 (over z, y, x), outer: 2 (over core).
Axes of the slice: x: 2, y: 2, z: 4, core: 2. Of those that a mesh axis runs over, the one named last changes fastest.
Arguments:
- feats_first: bfloat16 [2, 4096, 2048], P('outer', 'inner'), may hold values from -4 to 8
- feats_second: bfloat16 [2, 4096, 2048], P('outer', 'inner'), may hold values from -4 to 8
- expander: bfloat16 [2048, 1024], P('inner'), may hold values from -0.125 to 0.125
- tile_count: int32 [2, 16], replicated, may hold values from 64 to 256, as said below
- match_dev: int32 [2, 4096, 1], P('outer', 'inner'), may hold values from 0 to 15; in each aligned block of 256 rows (0 to 255, 256 to 511, ..., all dimensions but the last counted through in order) at most 48 rows name the same one
- match_tile: int32 [2, 4096], P('outer', 'inner'), may hold values from 0 to 255
Outputs:
- covariance: float32 [1024, 1024], P('inner')
- invariance: float32 [2, 4096], P('outer', 'inner')
Inputs may be any that keep to these rules, and one draw needn't show every extreme that they name: `tile_count`: for every slide some device has all 256 tiles live; the others at least a quarter. `match_dev`: at most 48 tiles of one device name the same device.
All inputs are finite; a program needn't handle non-finite values.
Results may differ from a plain program's by a relative error of at most 0.00135.
Values may be sent and summed in bfloat16 or wider, within the bound.
A program may use at most 64 MiB of HBM per device.

v0:
```python
import jax
import jax.numpy as jnp
from jax import lax
from jax.sharding import PartitionSpec as P


def shards(feats_first, feats_second, expander, tile_count, match_dev, match_tile):
    first_rows = feats_first[0]
    second_rows = feats_second[0]
    tile_rows = first_rows.shape[0]
    expand_width = expander.shape[1]
    group_size = lax.axis_size("inner")
    capacity = -(-max(2, 3 * tile_rows // group_size) // 16) * 16
    slots = group_size * capacity
    inner_pos = lax.axis_index("inner")
    outer_pos = lax.axis_index("outer")
    target_dev = match_dev[0, :, 0]
    target_tile = match_tile[0]
    row_index = jnp.arange(tile_rows, dtype=jnp.int32)
    same = (target_dev[:, None] == target_dev[None, :]) & (row_index[None, :] < row_index[:, None])
    slot_pos = jnp.sum(same.astype(jnp.int32), axis=1)
    slot = target_dev * capacity + slot_pos
    chosen = slot[:, None] == jnp.arange(slots, dtype=jnp.int32)[None, :]
    asked = jnp.sum(jnp.where(chosen, target_tile[:, None], 0), axis=0).reshape(
        group_size, capacity
    )
    wanted = lax.all_to_all(asked, "inner", split_axis=0, concat_axis=0, tiled=True).reshape(slots)
    piece = lax.all_gather(expander, "inner", axis=0, tiled=True)
    first_embed = jnp.dot(first_rows, piece, preferred_element_type=jnp.float32).astype(
        jnp.bfloat16
    )
    second_embed = jnp.dot(second_rows, piece, preferred_element_type=jnp.float32).astype(
        jnp.bfloat16
    )
    pick = (wanted[:, None] == row_index[None, :]).astype(jnp.bfloat16)
    send_rows = jnp.dot(pick, second_embed, preferred_element_type=jnp.float32).astype(jnp.bfloat16)
    recv_rows = lax.all_to_all(
        send_rows.reshape(group_size, capacity, expand_width),
        "inner",
        split_axis=0,
        concat_axis=0,
        tiled=True,
    ).reshape(slots, expand_width)
    partner = jnp.dot(chosen.astype(jnp.bfloat16), recv_rows, preferred_element_type=jnp.float32)
    counts = lax.dynamic_index_in_dim(tile_count, outer_pos, 0, keepdims=False)
    own_count = lax.dynamic_index_in_dim(counts, inner_pos, 0, keepdims=False)
    live = row_index < own_count
    dest_count = jnp.sum(
        jnp.where(
            target_dev[:, None] == jnp.arange(group_size, dtype=jnp.int32)[None, :],
            counts[None, :],
            0,
        ),
        axis=1,
    )
    valid = live & (target_tile < dest_count)
    diff = first_embed.astype(jnp.float32) - partner
    invariance = jnp.where(valid, jnp.mean(diff * diff, axis=-1), jnp.float32(0.0))
    masked = jnp.where(live[:, None], first_embed, jnp.zeros_like(first_embed))
    column_total = lax.psum(jnp.sum(masked.astype(jnp.float32), axis=0), ("inner", "outer"))
    total = jnp.sum(tile_count).astype(jnp.float32)
    share_rows = expand_width // group_size
    local_share = lax.psum_scatter(
        lax.dot_general(
            masked, masked, (((0,), (0,)), ((), ())), preferred_element_type=jnp.float32
        ),
        "inner",
        scatter_dimension=0,
        tiled=True,
    )
    gram_share = lax.psum(local_share, "outer")
    own_sums = lax.dynamic_slice_in_dim(column_total, inner_pos * share_rows, share_rows, 0)
    covariance = (gram_share - own_sums[:, None] * column_total[None, :] / total) / (total - 1.0)
    return (covariance, invariance[None, :])


def solution(mesh):
    return jax.shard_map(
        shards,
        mesh=mesh,
        in_specs=(
            P("outer", "inner", None),
            P("outer", "inner", None),
            P("inner", None),
            P(),
            P("outer", "inner", None),
            P("outer", "inner"),
        ),
        out_specs=(P("inner", None), P("outer", "inner")),
        check_vma=False,
    )
```

profile of v0, /device:TPU:0, one launch (start us, length us, event | category | flops | bytes accessed | tf_op | source)
XLA Modules:
  0.0 239.3 jit_solution(4994649485600865249)
XLA Ops:
  7.2 0.0 copy-start
  7.2 0.0 all-gather.2.cloned.1.call-start
  7.2 0.7 all-gather.2.cloned.1.call-update
  7.9 0.0 reduce-scatter.2.cloned.1.call-start
  8.0 1.3 dynamic_slice.11
  9.2 0.6 iota_compare_fusion.6
  9.9 79.7 %all-gather.2.cloned.1.call-done = bf16[2048,1024]{1,0:T(8,128)(2,1)} async-done(((bf16[128,1024]{1,0:T(8,128)(2,1)}), bf16[2048,1024]{1,0:T(8,128)(2,1)}) %all-gather.2.cloned.1.call-update) | async-done | bytes 4194320 | tf_op jit(solution)/shard_map/all_gather | solution.py:28
  89.6 3.8 %convert_reduce_fusion = (f32[1024]{0:T(1024)S(1)}, bf16[256,1024]{1,0:T(8,128)(2,1)S(1)}) fusion(pred[256]{0:T(512)(128)(4,1)S(1)} %iota_compare_fusion.6, bf16[2048,1024]{1,0:T(8,128)(2,1)} %all-gather.2.cloned.1.call-done, bf16[1,256,2048]{2,1,0:T(8,128)(2,1)} %param.6), kind=kOutput, calls=%fused_computation.8 | convolution fusion | flops 1074789376 | bytes 5771520 | tf_op jit(solution)/shard_map/dot_general | solution.py:29
  93.4 0.0 copy-start.1
  93.4 0.0 copy-start.2
  93.4 2.8 %fusion.8 = f32[1024,1024]{1,0:T(8,128)} fusion(bf16[256,1024]{1,0:T(8,128)(2,1)S(1)} %get-tuple-element.3, pred[256]{0:T(512)(128)(4,1)S(1)} %iota_compare_fusion.6), kind=kOutput, calls=%fused_computation.19 | convolution fusion | flops 537133056 | bytes 4718848 | tf_op jit(solution)/shard_map/dot_general | solution.py:64
  96.2 0.0 reduce-scatter.2.cloned.1.call-update
  96.2 0.0 copy-done.1
  96.2 0.2 convert_reduce_fusion.1
  96.4 0.0 copy-done.2
  96.4 0.2 select_reduce_fusion
  96.6 0.1 all_to_all.9
  96.7 11.4 %all_to_all.14 = s32[16,1,48]{2,1,0:T(1,128)S(1)} all-to-all(s32[16,1,48]{2,1,0:T(1,128)S(1)} %all_to_all.9), channel_id=1, replica_groups=mesh['inner'=16,'outer'=2] {'inner'}, dimensions={0} | all-to-all | bytes 6144 | tf_op jit(solution)/shard_map/all_to_all | solution.py:27
  108.0 0.5 broadcast.32
  108.5 0.7 reduce.3
  109.2 0.1 eq.66
  109.3 0.0 copy-done
  109.3 0.0 copy-start.3
  109.3 5.1 %convolution_convert_fusion = bf16[768,1024]{1,0:T(8,128)(2,1)} fusion(bf16[2048,1024]{1,0:T(8,128)(2,1)} %all-gather.2.cloned.1.call-done, bf16[1,256,2048]{2,1,0:T(8,128)(2,1)S(1)} %copy-done, s32[768]{0:T(1024)S(1)} %eq.66), kind=kOutput, calls=%fused_computation | convolution fusion | flops 1477640192 | bytes 6818816 | tf_op jit(solution)/shard_map/dot_general | solution.py:36
  114.4 3.8 %all-to-all-start.1 = ((bf16[16,48,1024]{2,1,0:T(8,128)(2,1)}), bf16[16,48,1024]{2,1,0:T(8,128)(2,1)S(1)}, u32[]{:S(2)}, u32[]{:S(2)}) async-start(bf16[16,48,1024]{2,1,0:T(8,128)(2,1)} %bitcast.22), calls=%async_computation.2 | async-start | bytes 3145728 | tf_op jit(solution)/shard_map/all_to_all | solution.py:37
  118.2 0.0 all-reduce.2.cloned.1.call-start
  118.3 0.0 copy-done.3
  118.3 0.6 reduce_sum.57
  119.6 0.1 select_reduce_fusion.1
  119.7 71.8 %psum.15 = f32[1024]{0:T(1024)S(1)} all-reduce(f32[1024]{0:T(1024)S(1)} %get-tuple-element.2), channel_id=1, replica_groups=mesh['inner'=16,'outer'=2] {'inner','outer'}, use_global_device_ids=true, to_apply=%region_3.4 | all-reduce | flops 1024 | bytes 8192 | tf_op jit(solution)/shard_map/psum | solution.py:60
  191.4 0.1 dynamic_slice.12
  191.5 0.0 all-to-all-done.1
  191.5 0.7 fusion.1
  192.3 19.4 %reduce-scatter.2.cloned.1.call-done = f32[64,1024]{1,0:T(8,128)} async-done(((f32[1024,1024]{1,0:T(8,128)}), f32[64,1024]{1,0:T(8,128)}) %reduce-scatter.2.cloned.1.call-update) | async-done | bytes 262160 | tf_op jit(solution)/shard_map/reduce_scatter | solution.py:63
  211.7 0.0 all-reduce.2.cloned.1.call-update
  211.7 1.2 and_select_fusion
  212.9 18.0 %all-reduce.2.cloned.1.call-done = f32[64,1024]{1,0:T(8,128)} async-done(((f32[64,1024]{1,0:T(8,128)}), f32[64,1024]{1,0:T(8,128)}) %all-reduce.2.cloned.1.call-update) | async-done | bytes 262160 | tf_op jit(solution)/shard_map/psum | solution.py:71
  231.0 1.8 subtract_divide_fusion
  (3 shorter events, 0.0 us)
Async XLA Ops:
  7.2 102.1 %copy-start = (bf16[1,256,2048]{2,1,0:T(8,128)(2,1)S(1)}, bf16[1,256,2048]{2,1,0:T(8,128)(2,1)}, u32[]{:S(2)}) copy-start(bf16[1,256,2048]{2,1,0:T(8,128)(2,1)} %param.7) | copy-start | bytes 3145732
  7.2 82.4 %all-gather.2.cloned.1.call-start = ((), (), s32[]{:S(2)}) async-start(), calls=%async_computation.3 | async-start | bytes 4456448 | tf_op jit(solution)/shard_map/all_gather | solution.py:28
  7.9 203.8 %reduce-scatter.2.cloned.1.call-start = ((), (), s32[]{:S(2)}) async-start(), calls=%async_computation.4 | async-start | bytes 4456448 | tf_op jit(solution)/shard_map/reduce_scatter | solution.py:63
  93.4 2.8 %copy-start.1 = (s32[1,256,1]{1,2,0:T(1,128)S(1)}, s32[1,256,1]{1,2,0:T(1,128)}, u32[]{:S(2)}) copy-start(s32[1,256,1]{1,2,0:T(1,128)} %param.10) | copy-start | bytes 3076
  93.4 3.0 %copy-start.2 = (s32[1,256]{1,0:T(1,128)S(1)}, s32[1,256]{1,0:T(1,128)}, u32[]{:S(2)}) copy-start(s32[1,256]{1,0:T(1,128)} %param.11) | copy-start | bytes 3076
  109.3 9.0 %copy-start.3 = (s32[2,16]{1,0:T(2,128)S(1)}, s32[2,16]{1,0:T(2,128)}, u32[]{:S(2)}) copy-start(s32[2,16]{1,0:T(2,128)} %param.9) | copy-start | bytes 388
  114.4 77.1 %all-to-all-start.1 = ((bf16[16,48,1024]{2,1,0:T(8,128)(2,1)}), bf16[16,48,1024]{2,1,0:T(8,128)(2,1)S(1)}, u32[]{:S(2)}, u32[]{:S(2)}) async-start(bf16[16,48,1024]{2,1,0:T(8,128)(2,1)} %bitcast.22), calls=%async_computation.2 | async-start | bytes 3145728 | tf_op jit(solution)/shard_map/all_to_all | solution.py:37
  118.2 112.8 %all-reduce.2.cloned.1.call-start = ((), (), s32[]{:S(2)}) async-start(), calls=%async_computation.5 | async-start | bytes 524288 | tf_op jit(solution)/shard_map/psum | solution.py:71
Sparse Core Ops, SparseCore 0:
  10.8 78.7 all-gather.1
  96.3 115.3 reduce-scatter.1
  214.0 16.9 all-reduce.1
where the time goes:
time: 240 us; the launch traced here: 239 us
  waiting for transfers between devices  118 us (49%)
  blocking collectives  83.1 us (35%)
  between operations  14.5 us (6%)
  matrix products  12.4 us (5%)
  other arithmetic  5.35 us (2%)
  starting transfers between devices  3.88 us (2%)
    all_gather x1, waiting for transfers between devices, shards(): piece = lax.all_gather(expander, 'inner', axis=0, tiled=True)  79.7 us
    psum x1, blocking collectives, shards(): lax.psum(jnp.sum(masked.astype(jnp.float32), axis=0), ('inner', 'outer'))  71.8 us
    reduce_scatter x1, waiting for transfers between devices, shards(): lax.psum_scatter(lax.dot_general(masked, masked, (((0,), (0,)), ((), ()))...  19.4 us
    psum x1, waiting for transfers between devices, shards(): gram_share = lax.psum(local_share, 'outer')  18 us
    all_to_all x1, blocking collectives, shards(): lax.all_to_all(asked, 'inner', split_axis=0, concat_axis=0, tiled=True)  11.4 us
    dot_general x1, matrix products, shards(): jnp.dot(pick, second_embed, preferred_element_type=jnp.float32)  5.14 us
  transfers between devices with their start and end apart: 4, of which 3 were waited for; matrix products, arithmetic and copies ran while one was open for 5% of the time, Pallas kernels for 0%

commit v1 on v0

--- a/solution.py
+++ b/solution.py
@@ -25,7 +25,23 @@
         group_size, capacity
     )
     wanted = lax.all_to_all(asked, "inner", split_axis=0, concat_axis=0, tiled=True).reshape(slots)
-    piece = lax.all_gather(expander, "inner", axis=0, tiled=True)
+    ways, here, turn = (lax.axis_size("inner"), lax.axis_index("inner"), expander.shape[0])
+    lengths = [n * ways if d == 0 else n for d, n in enumerate(expander.shape)]
+    full = lax.dynamic_update_slice_in_dim(
+        jnp.zeros(lengths, expander.dtype), expander, here * turn, axis=0
+    )
+    going_up = going_down = expander
+    for far in range(1, ways // 2 + 1):
+        going_up = lax.ppermute(going_up, "inner", [(d, (d + 1) % ways) for d in range(ways)])
+        full = lax.dynamic_update_slice_in_dim(full, going_up, (here - far) % ways * turn, axis=0)
+        if 2 * far < ways:
+            going_down = lax.ppermute(
+                going_down, "inner", [(d, (d - 1) % ways) for d in range(ways)]
+            )
+            full = lax.dynamic_update_slice_in_dim(
+                full, going_down, (here + far) % ways * turn, axis=0
+            )
+    piece = full
     first_embed = jnp.dot(first_rows, piece, preferred_element_type=jnp.float32).astype(
         jnp.bfloat16
     )

time: 240 us -> 262 us (1.092)
  starting transfers between devices: 3.88 us -> 57.9 us
  waiting for transfers between devices: 118 us -> 71.6 us
  local copies, waits for them, and re-layouts: 2.05 us -> 15.5 us
    all_gather x1 -> x0, waiting for transfers between devices: 79.7 us -> none  [shards(): piece = lax.all_gather(expander, 'inner', axis=0, tiled=True)]
    ppermute x0 -> x15, starting transfers between devices: none -> 54.1 us  [the longest x7 34.3 us: shards(): lax.ppermute(going_down, 'inner', [(d, (d - 1) % ways) for d in range(way...]
    ppermute x0 -> x15, waiting for transfers between devices: none -> 31.5 us  [the longest x8 30 us: shards(): lax.ppermute(going_up, 'inner', [(d, (d + 1) % ways) for d in range(ways)])]
    dynamic_update_slice x0 -> x16, local copies, waits for them, and re-layouts: none -> 11.6 us  [the longest x8 5.81 us: shards(): lax.dynamic_update_slice_in_dim(full, going_up, (here - far) % ways * tur...]
    all_to_all x1, blocking collectives: 11.4 us -> 14.7 us  [shards(): lax.all_to_all(asked, 'inner', split_axis=0, concat_axis=0, tiled=True)]
    psum x1, blocking collectives: 71.8 us -> 68.5 us  [shards(): lax.psum(jnp.sum(masked.astype(jnp.float32), axis=0), ('inner', 'outer'))]
  transfers between devices with their start and end apart: 4 -> 18, of which waited for: 3 -> 10; matrix products, arithmetic and copies ran while one was open for 5% -> 10% of each run, Pallas kernels for 0% -> 0%
where the time goes in v1:
time: 262 us
  blocking collectives  83.2 us (32%)
  waiting for transfers between devices  71.6 us (27%)
  starting transfers between devices  57.9 us (22%)
  local copies, waits for them, and re-layouts  15.5 us (6%)
  between operations  15.1 us (6%)
  matrix products  13 us (5%)
  other arithmetic  5.35 us (2%)
    psum x1, blocking collectives, shards(): lax.psum(jnp.sum(masked.astype(jnp.float32), axis=0), ('inner', 'outer'))  68.5 us
    ppermute x7, starting transfers between devices, shards(): lax.ppermute(going_down, 'inner', [(d, (d - 1) % ways) for d in range(way...  34.3 us
    ppermute x8, waiting for transfers between devices, shards(): lax.ppermute(going_up, 'inner', [(d, (d + 1) % ways) for d in range(ways)])  30 us
    reduce_scatter x1, waiting for transfers between devices, shards(): lax.psum_scatter(lax.dot_general(masked, masked, (((0,), (0,)), ((), ()))...  21.9 us
    ppermute x8, starting transfers between devices, shards(): lax.ppermute(going_up, 'inner', [(d, (d + 1) % ways) for d in range(ways)])  19.8 us
    psum x1, waiting for transfers between devices, shards(): gram_share = lax.psum(local_share, 'outer')  18.1 us
    all_to_all x1, blocking collectives, shards(): lax.all_to_all(asked, 'inner', split_axis=0, concat_axis=0, tiled=True)  14.7 us
    dot_general x1, matrix products, shards(): jnp.dot(pick, second_embed, preferred_element_type=jnp.float32)  5.88 us
  transfers between devices with their start and end apart: 18, of which 10 were waited for; matrix products, arithmetic and copies ran while one was open for 10% of the time, Pallas kernels for 0%

profile of v1, /device:TPU:0, one launch (start us, length us, event | category | flops | bytes accessed | tf_op | source)
XLA Modules:
  0.0 261.7 jit_solution(16351666387908890111)
XLA Ops:
  7.2 3.0 %collective-permute-start = (bf16[128,1024]{1,0:T(8,128)(2,1)}, bf16[128,1024]{1,0:T(8,128)(2,1)S(1)}, u32[]{:S(2)}, u32[]{:S(2)}) collective-permute-start(bf16[128,1024]{1,0:T(8,128)(2,1)} %param.8), channel_id=1, source_target_pairs={{0,2},{2,4},{4,6},{6,8},{8,10},{10,12},{12,14},{14,16},{16,18},{18... | collective-permute-start | bytes 786440 | tf_op jit(solution)/shard_map/ppermute | solution.py:35
  10.2 4.1 %collective-permute-start.1 = (bf16[128,1024]{1,0:T(8,128)(2,1)}, bf16[128,1024]{1,0:T(8,128)(2,1)S(1)}, u32[]{:S(2)}, u32[]{:S(2)}) collective-permute-start(bf16[128,1024]{1,0:T(8,128)(2,1)} %param.8), channel_id=1, source_target_pairs={{0,30},{2,0},{4,2},{6,4},{8,6},{10,8},{12,10},{14,12},{16,14},{18,... | collective-permute-start | bytes 786440 | tf_op jit(solution)/shard_map/ppermute | solution.py:38
  14.3 7.4 %collective-permute-done = bf16[128,1024]{1,0:T(8,128)(2,1)S(1)} collective-permute-done((bf16[128,1024]{1,0:T(8,128)(2,1)}, bf16[128,1024]{1,0:T(8,128)(2,1)S(1)}, u32[]{:S(2)}, u32[]{:S(2)}) %collective-permute-start) | collective-permute-done | bytes 262176 | tf_op jit(solution)/shard_map/ppermute | solution.py:35
  21.7 2.4 collective-permute-start.2
  24.1 3.2 %collective-permute-start.3 = (bf16[128,1024]{1,0:T(8,128)(2,1)S(1)}, bf16[128,1024]{1,0:T(8,128)(2,1)S(1)}, u32[]{:S(2)}, u32[]{:S(2)}) collective-permute-start(bf16[128,1024]{1,0:T(8,128)(2,1)S(1)} %collective-permute-done.1), channel_id=1, source_target_pairs={{0,30},{2,0},{4,2},{6,4},{8,6},{10,8},{12,10},{14,12},{16,14},{18,... | collective-permute-start | bytes 786440 | tf_op jit(solution)/shard_map/ppermute | solution.py:38
  27.4 7.1 %collective-permute-done.2 = bf16[128,1024]{1,0:T(8,128)(2,1)S(1)} collective-permute-done((bf16[128,1024]{1,0:T(8,128)(2,1)S(1)}, bf16[128,1024]{1,0:T(8,128)(2,1)S(1)}, u32[]{:S(2)}, u32[]{:S(2)}) %collective-permute-start.2) | collective-permute-done | bytes 262176 | tf_op jit(solution)/shard_map/ppermute | solution.py:35
  34.4 2.5 collective-permute-start.4
  36.9 4.7 %collective-permute-start.5 = (bf16[128,1024]{1,0:T(8,128)(2,1)S(1)}, bf16[128,1024]{1,0:T(8,128)(2,1)S(1)}, u32[]{:S(2)}, u32[]{:S(2)}) collective-permute-start(bf16[128,1024]{1,0:T(8,128)(2,1)S(1)} %collective-permute-done.3), channel_id=1, source_target_pairs={{0,30},{2,0},{4,2},{6,4},{8,6},{10,8},{12,10},{14,12},{16,14},{18,... | collective-permute-start | bytes 786440 | tf_op jit(solution)/shard_map/ppermute | solution.py:38
  41.6 2.5 broadcast_in_dim.58
  45.4 0.9 collective-permute-done.4
  46.3 2.5 collective-permute-start.6
  49.7 0.7 constant_dynamic-update-slice_fusion.14
  50.5 4.9 %collective-permute-start.7 = (bf16[128,1024]{1,0:T(8,128)(2,1)S(1)}, bf16[128,1024]{1,0:T(8,128)(2,1)S(1)}, u32[]{:S(2)}, u32[]{:S(2)}) collective-permute-start(bf16[128,1024]{1,0:T(8,128)(2,1)S(1)} %collective-permute-done.5), channel_id=1, source_target_pairs={{0,30},{2,0},{4,2},{6,4},{8,6},{10,8},{12,10},{14,12},{16,14},{18,... | collective-permute-start | bytes 786440 | tf_op jit(solution)/shard_map/ppermute | solution.py:38
  56.1 3.6 %collective-permute-done.6 = bf16[128,1024]{1,0:T(8,128)(2,1)S(1)} collective-permute-done((bf16[128,1024]{1,0:T(8,128)(2,1)S(1)}, bf16[128,1024]{1,0:T(8,128)(2,1)S(1)}, u32[]{:S(2)}, u32[]{:S(2)}) %collective-permute-start.6) | collective-permute-done | bytes 262176 | tf_op jit(solution)/shard_map/ppermute | solution.py:35
  59.7 2.5 collective-permute-start.8
  62.2 0.7 constant_dynamic-update-slice_fusion.12
  62.9 0.7 constant_dynamic-update-slice_fusion.11
  63.6 5.6 %collective-permute-start.9 = (bf16[128,1024]{1,0:T(8,128)(2,1)S(1)}, bf16[128,1024]{1,0:T(8,128)(2,1)S(1)}, u32[]{:S(2)}, u32[]{:S(2)}) collective-permute-start(bf16[128,1024]{1,0:T(8,128)(2,1)S(1)} %collective-permute-done.7), channel_id=1, source_target_pairs={{0,30},{2,0},{4,2},{6,4},{8,6},{10,8},{12,10},{14,12},{16,14},{18,... | collective-permute-start | bytes 786440 | tf_op jit(solution)/shard_map/ppermute | solution.py:38
  69.9 2.9 %collective-permute-done.8 = bf16[128,1024]{1,0:T(8,128)(2,1)S(1)} collective-permute-done((bf16[128,1024]{1,0:T(8,128)(2,1)S(1)}, bf16[128,1024]{1,0:T(8,128)(2,1)S(1)}, u32[]{:S(2)}, u32[]{:S(2)}) %collective-permute-start.8) | collective-permute-done | bytes 262176 | tf_op jit(solution)/shard_map/ppermute | solution.py:35
  72.8 2.5 collective-permute-start.10
  75.3 0.7 constant_dynamic-update-slice_fusion.9
  76.0 0.7 constant_dynamic-update-slice_fusion.8
  76.7 5.6 %collective-permute-start.11 = (bf16[128,1024]{1,0:T(8,128)(2,1)S(1)}, bf16[128,1024]{1,0:T(8,128)(2,1)S(1)}, u32[]{:S(2)}, u32[]{:S(2)}) collective-permute-start(bf16[128,1024]{1,0:T(8,128)(2,1)S(1)} %collective-permute-done.9), channel_id=1, source_target_pairs={{0,30},{2,0},{4,2},{6,4},{8,6},{10,8},{12,10},{14,12},{16,14},{18,... | collective-permute-start | bytes 786440 | tf_op jit(solution)/shard_map/ppermute | solution.py:38
  82.3 0.7 constant_dynamic-update-slice_fusion.7
  83.1 2.3 collective-permute-done.10
  85.3 2.5 collective-permute-start.12
  87.8 0.7 constant_dynamic-update-slice_fusion.6
  88.5 0.7 constant_dynamic-update-slice_fusion.5
  89.3 6.2 %collective-permute-start.13 = (bf16[128,1024]{1,0:T(8,128)(2,1)S(1)}, bf16[128,1024]{1,0:T(8,128)(2,1)S(1)}, u32[]{:S(2)}, u32[]{:S(2)}) collective-permute-start(bf16[128,1024]{1,0:T(8,128)(2,1)S(1)} %collective-permute-done.11), channel_id=1, source_target_pairs={{0,30},{2,0},{4,2},{6,4},{8,6},{10,8},{12,10},{14,12},{16,14},{18,... | collective-permute-start | bytes 786440 | tf_op jit(solution)/shard_map/ppermute | solution.py:38
  95.5 0.7 constant_dynamic-update-slice_fusion.4
  96.3 2.1 collective-permute-start.14
  98.3 0.7 constant_dynamic-update-slice_fusion.3
  99.1 0.7 constant_dynamic-update-slice_fusion.2
  99.8 1.5 collective-permute-done.13
  101.3 0.7 constant_dynamic-update-slice_fusion.1
  102.0 5.8 %collective-permute-done.14 = bf16[128,1024]{1,0:T(8,128)(2,1)S(1)} collective-permute-done((bf16[128,1024]{1,0:T(8,128)(2,1)S(1)}, bf16[128,1024]{1,0:T(8,128)(2,1)S(1)}, u32[]{:S(2)}, u32[]{:S(2)}) %collective-permute-start.14) | collective-permute-done | bytes 262176 | tf_op jit(solution)/shard_map/ppermute | solution.py:35
  107.8 0.7 constant_dynamic-update-slice_fusion
  108.6 3.6 %convert_reduce_fusion = (f32[1024]{0:T(1024)S(1)}, bf16[1024,256]{1,0:T(8,128)(2,1)S(1)}) fusion(pred[256]{0:T(512)(128)(4,1)S(1)} %iota_compare_fusion.8, bf16[2048,1024]{1,0:T(8,128)(2,1)} %constant_dynamic-update-slice_fusion, bf16[1,256,2048]{2,1,0:T(8,128)(2,1)S(1)} %copy-done.5), kind=kOutput, calls=%fused_computation.8 | convolution fusion | flops 1074789376 | bytes 5771520 | tf_op jit(solution)/shard_map/dot_general | solution.py:45
  112.2 2.7 %fusion.6 = f32[1024,1024]{1,0:T(8,128)} fusion(bf16[1024,256]{1,0:T(8,128)(2,1)S(1)} %get-tuple-element.3, pred[256]{0:T(512)(128)(4,1)S(1)} %iota_compare_fusion.8), kind=kOutput, calls=%fused_computation.14 | convolution fusion | flops 537133056 | bytes 4718848 | tf_op jit(solution)/shard_map/dot_general | solution.py:80
  115.4 14.7 %all_to_all.14 = s32[16,1,48]{2,1,0:T(1,128)S(1)} all-to-all(s32[16,1,48]{2,1,0:T(1,128)S(1)} %all_to_all.9), channel_id=1, replica_groups=mesh['inner'=16,'outer'=2] {'inner'}, dimensions={0} | all-to-all | bytes 6144 | tf_op jit(solution)/shard_map/all_to_all | solution.py:27
  131.3 5.9 %convolution_convert_fusion = bf16[768,1024]{1,0:T(8,128)(2,1)} fusion(bf16[2048,1024]{1,0:T(8,128)(2,1)} %constant_dynamic-update-slice_fusion, bf16[1,256,2048]{2,1,0:T(8,128)(2,1)S(1)} %copy-done, s32[768]{0:T(1024)S(1)} %eq.82), kind=kOutput, calls=%fused_computation | convolution fusion | flops 1477640192 | bytes 6818816 | tf_op jit(solution)/shard_map/dot_general | solution.py:52
  137.2 3.7 %all-to-all-start.1 = ((bf16[16,48,1024]{2,1,0:T(8,128)(2,1)}), bf16[16,48,1024]{2,1,0:T(8,128)(2,1)S(1)}, u32[]{:S(2)}, u32[]{:S(2)}) async-start(bf16[16,48,1024]{2,1,0:T(8,128)(2,1)} %bitcast.28), calls=%async_computation.2 | async-start | bytes 3145728 | tf_op jit(solution)/shard_map/all_to_all | solution.py:53
  142.4 68.5 %psum.15 = f32[1024]{0:T(1024)S(1)} all-reduce(f32[1024]{0:T(1024)S(1)} %get-tuple-element.2), channel_id=1, replica_groups=mesh['inner'=16,'outer'=2] {'inner','outer'}, use_global_device_ids=true, to_apply=%region_3.4 | all-reduce | flops 1024 | bytes 8192 | tf_op jit(solution)/shard_map/psum | solution.py:76
  211.0 0.8 fusion.3
  211.8 21.9 %reduce-scatter.2.cloned.1.call-done = f32[64,1024]{1,0:T(8,128)} async-done(((f32[1024,1024]{1,0:T(8,128)}), f32[64,1024]{1,0:T(8,128)}) %reduce-scatter.2.cloned.1.call-update) | async-done | bytes 262160 | tf_op jit(solution)/shard_map/reduce_scatter | solution.py:79
  233.7 1.2 and_select_fusion
  234.9 18.1 %all-reduce.2.cloned.1.call-done = f32[64,1024]{1,0:T(8,128)} async-done(((f32[64,1024]{1,0:T(8,128)}), f32[64,1024]{1,0:T(8,128)}) %all-reduce.2.cloned.1.call-update) | async-done | bytes 262160 | tf_op jit(solution)/shard_map/psum | solution.py:87
  253.1 1.8 subtract_divide_fusion
  (41 shorter events, 6.0 us)
Async XLA Ops:
  7.2 124.1 %copy-start = (bf16[1,256,2048]{2,1,0:T(8,128)(2,1)S(1)}, bf16[1,256,2048]{2,1,0:T(8,128)(2,1)}, u32[]{:S(2)}) copy-start(bf16[1,256,2048]{2,1,0:T(8,128)(2,1)} %param.7) | copy-start | bytes 3145732
  7.2 36.9 %copy-start.1 = (bf16[128,1024]{1,0:T(8,128)(2,1)S(1)}, bf16[128,1024]{1,0:T(8,128)(2,1)}, u32[]{:S(2)}) copy-start(bf16[128,1024]{1,0:T(8,128)(2,1)} %param.8) | copy-start | bytes 786436
  7.2 37.6 %copy-start.4 = (s32[2,16]{1,0:T(2,128)S(1)}, s32[2,16]{1,0:T(2,128)}, u32[]{:S(2)}) copy-start(s32[2,16]{1,0:T(2,128)} %param.9) | copy-start | bytes 388
  7.2 226.5 %reduce-scatter.2.cloned.1.call-start = ((), (), s32[]{:S(2)}) async-start(), calls=%async_computation.3 | async-start | bytes 4456448 | tf_op jit(solution)/shard_map/reduce_scatter | solution.py:79
  7.2 14.5 %collective-permute-start = (bf16[128,1024]{1,0:T(8,128)(2,1)}, bf16[128,1024]{1,0:T(8,128)(2,1)S(1)}, u32[]{:S(2)}, u32[]{:S(2)}) collective-permute-start(bf16[128,1024]{1,0:T(8,128)(2,1)} %param.8), channel_id=1, source_target_pairs={{0,2},{2,4},{4,6},{6,8},{8,10},{10,12},{12,14},{14,16},{16,18},{18... | collective-permute-start | bytes 786440 | tf_op jit(solution)/shard_map/ppermute | solution.py:35
  10.2 13.9 %collective-permute-start.1 = (bf16[128,1024]{1,0:T(8,128)(2,1)}, bf16[128,1024]{1,0:T(8,128)(2,1)S(1)}, u32[]{:S(2)}, u32[]{:S(2)}) collective-permute-start(bf16[128,1024]{1,0:T(8,128)(2,1)} %param.8), channel_id=1, source_target_pairs={{0,30},{2,0},{4,2},{6,4},{8,6},{10,8},{12,10},{14,12},{16,14},{18,... | collective-permute-start | bytes 786440 | tf_op jit(solution)/shard_map/ppermute | solution.py:38
  21.7 12.7 %collective-permute-start.2 = (bf16[128,1024]{1,0:T(8,128)(2,1)S(1)}, bf16[128,1024]{1,0:T(8,128)(2,1)S(1)}, u32[]{:S(2)}, u32[]{:S(2)}) collective-permute-start(bf16[128,1024]{1,0:T(8,128)(2,1)S(1)} %collective-permute-done), channel_id=1, source_target_pairs={{0,2},{2,4},{4,6},{6,8},{8,10},{10,12},{12,14},{14,16},{16,18},{18... | collective-permute-start | bytes 786440 | tf_op jit(solution)/shard_map/ppermute | solution.py:35
  24.1 12.8 %collective-permute-start.3 = (bf16[128,1024]{1,0:T(8,128)(2,1)S(1)}, bf16[128,1024]{1,0:T(8,128)(2,1)S(1)}, u32[]{:S(2)}, u32[]{:S(2)}) collective-permute-start(bf16[128,1024]{1,0:T(8,128)(2,1)S(1)} %collective-permute-done.1), channel_id=1, source_target_pairs={{0,30},{2,0},{4,2},{6,4},{8,6},{10,8},{12,10},{14,12},{16,14},{18,... | collective-permute-start | bytes 786440 | tf_op jit(solution)/shard_map/ppermute | solution.py:38
  34.4 11.9 %collective-permute-start.4 = (bf16[128,1024]{1,0:T(8,128)(2,1)S(1)}, bf16[128,1024]{1,0:T(8,128)(2,1)S(1)}, u32[]{:S(2)}, u32[]{:S(2)}) collective-permute-start(bf16[128,1024]{1,0:T(8,128)(2,1)S(1)} %collective-permute-done.2), channel_id=1, source_target_pairs={{0,2},{2,4},{4,6},{6,8},{8,10},{10,12},{12,14},{14,16},{16,18},{18... | collective-permute-start | bytes 786440 | tf_op jit(solution)/shard_map/ppermute | solution.py:35
  36.9 13.6 %collective-permute-start.5 = (bf16[128,1024]{1,0:T(8,128)(2,1)S(1)}, bf16[128,1024]{1,0:T(8,128)(2,1)S(1)}, u32[]{:S(2)}, u32[]{:S(2)}) collective-permute-start(bf16[128,1024]{1,0:T(8,128)(2,1)S(1)} %collective-permute-done.3), channel_id=1, source_target_pairs={{0,30},{2,0},{4,2},{6,4},{8,6},{10,8},{12,10},{14,12},{16,14},{18,... | collective-permute-start | bytes 786440 | tf_op jit(solution)/shard_map/ppermute | solution.py:38
  46.3 13.4 %collective-permute-start.6 = (bf16[128,1024]{1,0:T(8,128)(2,1)S(1)}, bf16[128,1024]{1,0:T(8,128)(2,1)S(1)}, u32[]{:S(2)}, u32[]{:S(2)}) collective-permute-start(bf16[128,1024]{1,0:T(8,128)(2,1)S(1)} %collective-permute-done.4), channel_id=1, source_target_pairs={{0,2},{2,4},{4,6},{6,8},{8,10},{10,12},{12,14},{14,16},{16,18},{18... | collective-permute-start | bytes 786440 | tf_op jit(solution)/shard_map/ppermute | solution.py:35
  49.7 58.9 %copy-start.5 = (bf16[1,256,2048]{2,1,0:T(8,128)(2,1)S(1)}, bf16[1,256,2048]{2,1,0:T(8,128)(2,1)}, u32[]{:S(2)}) copy-start(bf16[1,256,2048]{2,1,0:T(8,128)(2,1)} %param.6) | copy-start | bytes 3145732
  50.5 13.2 %collective-permute-start.7 = (bf16[128,1024]{1,0:T(8,128)(2,1)S(1)}, bf16[128,1024]{1,0:T(8,128)(2,1)S(1)}, u32[]{:S(2)}, u32[]{:S(2)}) collective-permute-start(bf16[128,1024]{1,0:T(8,128)(2,1)S(1)} %collective-permute-done.5), channel_id=1, source_target_pairs={{0,30},{2,0},{4,2},{6,4},{8,6},{10,8},{12,10},{14,12},{16,14},{18,... | collective-permute-start | bytes 786440 | tf_op jit(solution)/shard_map/ppermute | solution.py:38
  59.7 13.1 %collective-permute-start.8 = (bf16[128,1024]{1,0:T(8,128)(2,1)S(1)}, bf16[128,1024]{1,0:T(8,128)(2,1)S(1)}, u32[]{:S(2)}, u32[]{:S(2)}) collective-permute-start(bf16[128,1024]{1,0:T(8,128)(2,1)S(1)} %collective-permute-done.6), channel_id=1, source_target_pairs={{0,2},{2,4},{4,6},{6,8},{8,10},{10,12},{12,14},{14,16},{16,18},{18... | collective-permute-start | bytes 786440 | tf_op jit(solution)/shard_map/ppermute | solution.py:35
  63.6 13.1 %collective-permute-start.9 = (bf16[128,1024]{1,0:T(8,128)(2,1)S(1)}, bf16[128,1024]{1,0:T(8,128)(2,1)S(1)}, u32[]{:S(2)}, u32[]{:S(2)}) collective-permute-start(bf16[128,1024]{1,0:T(8,128)(2,1)S(1)} %collective-permute-done.7), channel_id=1, source_target_pairs={{0,30},{2,0},{4,2},{6,4},{8,6},{10,8},{12,10},{14,12},{16,14},{18,... | collective-permute-start | bytes 786440 | tf_op jit(solution)/shard_map/ppermute | solution.py:38
  72.8 12.6 %collective-permute-start.10 = (bf16[128,1024]{1,0:T(8,128)(2,1)S(1)}, bf16[128,1024]{1,0:T(8,128)(2,1)S(1)}, u32[]{:S(2)}, u32[]{:S(2)}) collective-permute-start(bf16[128,1024]{1,0:T(8,128)(2,1)S(1)} %collective-permute-done.8), channel_id=1, source_target_pairs={{0,2},{2,4},{4,6},{6,8},{8,10},{10,12},{12,14},{14,16},{16,18},{18... | collective-permute-start | bytes 786440 | tf_op jit(solution)/shard_map/ppermute | solution.py:35
  76.7 12.6 %collective-permute-start.11 = (bf16[128,1024]{1,0:T(8,128)(2,1)S(1)}, bf16[128,1024]{1,0:T(8,128)(2,1)S(1)}, u32[]{:S(2)}, u32[]{:S(2)}) collective-permute-start(bf16[128,1024]{1,0:T(8,128)(2,1)S(1)} %collective-permute-done.9), channel_id=1, source_target_pairs={{0,30},{2,0},{4,2},{6,4},{8,6},{10,8},{12,10},{14,12},{16,14},{18,... | collective-permute-start | bytes 786440 | tf_op jit(solution)/shard_map/ppermute | solution.py:38
  85.3 10.9 %collective-permute-start.12 = (bf16[128,1024]{1,0:T(8,128)(2,1)S(1)}, bf16[128,1024]{1,0:T(8,128)(2,1)S(1)}, u32[]{:S(2)}, u32[]{:S(2)}) collective-permute-start(bf16[128,1024]{1,0:T(8,128)(2,1)S(1)} %collective-permute-done.10), channel_id=1, source_target_pairs={{0,2},{2,4},{4,6},{6,8},{8,10},{10,12},{12,14},{14,16},{16,18},{18... | collective-permute-start | bytes 786440 | tf_op jit(solution)/shard_map/ppermute | solution.py:35
  89.3 12.0 %collective-permute-start.13 = (bf16[128,1024]{1,0:T(8,128)(2,1)S(1)}, bf16[128,1024]{1,0:T(8,128)(2,1)S(1)}, u32[]{:S(2)}, u32[]{:S(2)}) collective-permute-start(bf16[128,1024]{1,0:T(8,128)(2,1)S(1)} %collective-permute-done.11), channel_id=1, source_target_pairs={{0,30},{2,0},{4,2},{6,4},{8,6},{10,8},{12,10},{14,12},{16,14},{18,... | collective-permute-start | bytes 786440 | tf_op jit(solution)/shard_map/ppermute | solution.py:38
  96.3 11.6 %collective-permute-start.14 = (bf16[128,1024]{1,0:T(8,128)(2,1)S(1)}, bf16[128,1024]{1,0:T(8,128)(2,1)S(1)}, u32[]{:S(2)}, u32[]{:S(2)}) collective-permute-start(bf16[128,1024]{1,0:T(8,128)(2,1)S(1)} %collective-permute-done.12), channel_id=1, source_target_pairs={{0,2},{2,4},{4,6},{6,8},{8,10},{10,12},{12,14},{14,16},{16,18},{18... | collective-permute-start | bytes 786440 | tf_op jit(solution)/shard_map/ppermute | solution.py:35
  112.2 2.7 %copy-start.2 = (s32[1,256,1]{1,2,0:T(1,128)S(1)}, s32[1,256,1]{1,2,0:T(1,128)}, u32[]{:S(2)}) copy-start(s32[1,256,1]{1,2,0:T(1,128)} %param.10) | copy-start | bytes 3076
  112.2 2.9 %copy-start.3 = (s32[1,256]{1,0:T(1,128)S(1)}, s32[1,256]{1,0:T(1,128)}, u32[]{:S(2)}) copy-start(s32[1,256]{1,0:T(1,128)} %param.11) | copy-start | bytes 3076
  137.2 73.8 %all-to-all-start.1 = ((bf16[16,48,1024]{2,1,0:T(8,128)(2,1)}), bf16[16,48,1024]{2,1,0:T(8,128)(2,1)S(1)}, u32[]{:S(2)}, u32[]{:S(2)}) async-start(bf16[16,48,1024]{2,1,0:T(8,128)(2,1)} %bitcast.28), calls=%async_computation.2 | async-start | bytes 3145728 | tf_op jit(solution)/shard_map/all_to_all | solution.py:53
  140.9 112.1 %all-reduce.2.cloned.1.call-start = ((), (), s32[]{:S(2)}) async-start(), calls=%async_computation.4 | async-start | bytes 524288 | tf_op jit(solution)/shard_map/psum | solution.py:87
Sparse Core Ops, SparseCore 0:
  115.0 118.5 reduce-scatter.1
  236.0 17.0 all-reduce.1
